TPU v7x, 512 devices: a whole 4x8x8 slice. The times are simulated.
512 devices in a mesh: ew: 32 (over z, x), ns: 16 (over y, core).
Axes of the slice: x: 4, y: 8, z: 8, core: 2. Of those that a mesh axis runs over, the one named last changes fastest.
Arguments:
- grid: bfloat16 [32, 2, 1280, 5152], P(None, None, 'ns', 'ew'), may hold values from -6 to 6
- band_rows: int32 [1280], replicated, may hold values from 0 to 1279, each once
- wave_pairs: int32 [16], replicated, may hold values from 0 to 323, as said below
- packer_order: int32 [32], replicated, may hold values from 0 to 31, each once
- field_bits: int32 [4], replicated, may hold values from 10 to 14
- field_power: float32 [4], replicated, may hold values from -0.6 to 0.6
- legendre: float32 [16, 1280, 649], P('ns'), may hold values from -0.15625 to 0.15625
Outputs:
- packed: float32 [32, 16, 2, 649], P('ew', 'ns')
Inputs may be any that keep to these rules, and one draw needn't show every extreme that they name: `wave_pairs`: distinct values.
All inputs are finite; a program needn't handle non-finite values.
Results may differ from a plain program's by a relative error of at most 0.0003.
Values sent between devices are 32-bit elements; how exact they have to be, the bound alone decides.
A program may use at most 64 MiB of HBM per device.

v0:
```python
import jax
import jax.numpy as jnp
from jax import lax
from jax.sharding import PartitionSpec as P


def in_blocks(shard, dim, size):
    before, after = (shard.shape[:dim], shard.shape[dim + 1 :])
    return jnp.moveaxis(shard.reshape(*before, size, -1, *after), dim, 0)


def sum_at_owner(shard, axis, dim):
    size = lax.axis_size(axis)
    tiles = lax.all_to_all(in_blocks(shard, dim, size), axis, 0, 0, tiled=True)
    return jnp.sum(tiles, axis=0)


def sent_to_all(shard, axis):
    size = lax.axis_size(axis)
    return lax.all_to_all(
        jnp.broadcast_to(shard[None], (size, *shard.shape)), axis, 0, 0, tiled=True
    )


def of_everyone(shard, axis):
    return sent_to_all(shard, axis).max(axis=0)


def in_one(arrays, axis):
    ends = [0]
    for a in arrays:
        ends.append(ends[-1] + a.size)
    subtotal = of_everyone(jnp.concatenate([a.ravel() for a in arrays]), axis)
    return tuple((subtotal[b:e].reshape(a.shape) for a, b, e in zip(arrays, ends, ends[1:])))


def cycle_table(lat_ids, first_point, point_count, wave_list, truncation):
    lengths = 20 + 4 * lat_ids
    points = first_point + jnp.arange(point_count, dtype=jnp.int32)
    numbers = jnp.stack([wave_list, truncation - wave_list], 1).reshape(-1)
    product = numbers[None, None, :] * points[None, :, None] % lengths[:, None, None]
    length_f = lengths.astype(jnp.float32)[:, None, None]
    angles = product.astype(jnp.float32) * (6.283185307179586 / length_f)
    inside = points[None, :, None] < lengths[:, None, None]
    factor = jnp.where(inside, 1.0 / length_f, jnp.float32(0.0))
    trig_values = jnp.stack([jnp.cos(angles) * factor, -jnp.sin(angles) * factor], -1)
    return trig_values.reshape(lat_ids.shape[0], point_count, -1)


def coefficients(ordered, legendre, wave_list, truncation, powers):
    symmetric = ordered[:, 0] + ordered[:, 1]
    antisym = ordered[:, 0] - ordered[:, 1]
    slots, nlat, width = symmetric.shape
    pcount = width // 4
    stacked = jnp.concatenate(
        [symmetric.reshape(slots, nlat, pcount, 4), antisym.reshape(slots, nlat, pcount, 4)], -1
    )
    result = jnp.einsum("prc,frpq->fpqc", legendre, stacked, precision=lax.Precision.HIGHEST)
    columns = jnp.arange(legendre.shape[2], dtype=jnp.int32)[None, :]
    wavenum = wave_list[:, None]
    first_part = columns <= truncation - wavenum
    shifted = columns - (truncation - wavenum + 1)
    even_parity = jnp.where(first_part, columns % 2 == 0, shifted % 2 == 0)
    halves = []
    for e in (0, 1):
        chosen = jnp.where(
            first_part,
            jnp.where(even_parity, result[:, :, e], result[:, :, 4 + e]),
            jnp.where(even_parity, result[:, :, 2 + e], result[:, :, 6 + e]),
        )
        halves.append(chosen)
    coefficient = jnp.stack(halves, 2)
    degree = jnp.where(first_part, wavenum + columns, columns - 1).astype(jnp.float32)
    logs = jnp.log(degree * (degree + 1.0) + 2.0)
    weight = jnp.exp(powers[:, None, None] * logs[None, :, :])
    return coefficient * weight[:, :, None, :]


def slot_settings(slot_fields, field_bits, field_power, levels):
    field_type = slot_fields // levels
    onehot = field_type[:, None] == jnp.arange(field_bits.shape[0], dtype=jnp.int32)[None, :]
    powers = jnp.sum(jnp.where(onehot, field_power[None, :], jnp.float32(0.0)), -1)
    bit_count = jnp.sum(jnp.where(onehot, field_bits[None, :], 0), -1).astype(jnp.float32)
    return (powers, (jnp.exp2(bit_count) - 1.0) / 4096.0)


def pack_values(scaled, lowest, highest, spread):
    span = highest - lowest + 1e-06
    return (
        (scaled - lowest[:, None, None, None])
        / span[:, None, None, None]
        * spread[:, None, None, None]
    )


def segment_terms_of(picked_rows, trig_values):
    return jnp.einsum(
        "fhrk,rkc->fhrc",
        picked_rows.astype(jnp.float32),
        trig_values,
        precision=lax.Precision.HIGHEST,
    )


def shards(grid, band_rows, wave_pairs, packer_order, field_bits, field_power, legendre):
    band_size = grid.shape[2]
    segment = grid.shape[3]
    total_slots = grid.shape[0]
    fl_dev = total_slots // lax.axis_size("ew")
    pair_dev = legendre.shape[0]
    truncation = legendre.shape[2] - 2
    levels = total_slots // field_bits.shape[0]
    ns_index = lax.axis_index("ns")
    ew_index = lax.axis_index("ew")
    lat_ids = lax.dynamic_slice_in_dim(band_rows, ns_index * band_size, band_size)
    trig_values = cycle_table(lat_ids, ew_index * segment, segment, wave_pairs, truncation)
    summed = sum_at_owner(
        segment_terms_of(jnp.take(grid, packer_order, axis=0), trig_values), "ew", 0
    )
    ordered = lax.all_to_all(summed, "ns", split_axis=3, concat_axis=2, tiled=True)
    local_waves = lax.dynamic_slice_in_dim(wave_pairs, ns_index * pair_dev, pair_dev)
    local_fields = lax.dynamic_slice_in_dim(packer_order, ew_index * fl_dev, fl_dev)
    powers, spread = slot_settings(local_fields, field_bits, field_power, levels)
    scaled = coefficients(ordered, legendre, local_waves, truncation, powers)
    local_high = jnp.max(scaled, axis=(1, 2, 3))
    local_low = jnp.min(scaled, axis=(1, 2, 3))
    highest, negated = in_one((local_high, -local_low), "ns")
    lowest = -negated
    return pack_values(scaled, lowest, highest, spread)


def solution(mesh):
    return jax.shard_map(
        shards,
        mesh=mesh,
        in_specs=(P(None, None, "ns", "ew"), P(), P(), P(), P(), P(), P("ns", None, None)),
        out_specs=P("ew", "ns", None, None),
        check_vma=False,
    )
```

profile of v0, /device:TPU:1, one launch (start us, length us, event | category | flops | bytes accessed | tf_op | source)
XLA Modules:
  0.0 165.9 jit_solution(11019741589729450771)
XLA Ops:
  0.0 0.0 copy-start
  0.0 0.9 broadcast_compare_fusion
  0.9 0.7 compare_select_fusion.4
  1.6 0.7 compare_and_fusion
  2.3 0.7 subtract_bitcast_fusion.1
  2.9 0.7 pad_add_fusion
  3.6 0.1 copy.43
  3.7 0.1 mul.142
  3.8 0.1 compare_select_fusion
  3.9 0.1 broadcast_multiply_fusion
  3.9 34.9 %fusion.9 = (f32[80,161,32,1]{1,2,3,0:T(8,128)S(1)}, f32[80,161,32,1]{1,2,3,0:T(8,128)S(1)}) fusion(f32[80,161]{1,0:T(8,128)S(1)} %compare_select_fusion, f32[80]{0:T(128)S(1)} %get-tuple-element.18, s32[80]{0:T(128)S(1)} %compare_select_fusion.5, s32[161,32]{0,1:T(8,128)S(1)} %broadcast_multiply_fusion, pred[80]{0:T(512)(128)(4,1)S(1)} %get-tuple-element.8), kind=kLoop, calls=%fused_computation.15 | loop fusion | flops 4945920 | bytes 3370128 | tf_op jit(solution)/shard_map/mul | solution.py:46
  38.9 1.0 pad_maximum_fusion
  39.8 5.3 %copy.44 = f32[80,161,32,2]{1,0,3,2:T(8,128)} copy(f32[80,161,32,2]{1,2,3,0:T(8,128)S(1)} %pad_maximum_fusion) | data formatting | bytes 6594560 | tf_op jit(solution)/shard_map/stack | solution.py:46
  45.2 0.0 copy-done
  45.2 2.2 %gather_fusion = bf16[32,2,80,161]{3,2,1,0:T(8,128)(2,1)} fusion(bf16[32,2,80,161]{3,2,1,0:T(8,128)(2,1)S(1)} %copy-done, s32[1024]{0:T(1024)S(1)} %pad_clamp_fusion), kind=kCustom, calls=%fused_computation | custom fusion | bytes 3297408 | tf_op jit(solution)/shard_map/jit(_take)/gather | solution.py:118
  47.4 0.0 copy-start.1
  47.4 2.2 %broadcast_select_fusion = bf16[32,2,80,161]{3,2,1,0:T(8,128)(2,1)S(1)} fusion(bf16[32,2,80,161]{3,2,1,0:T(8,128)(2,1)} %gather_fusion, pred[32]{0:T(512)(128)(4,1)S(1)} %compare_and_fusion), kind=kLoop, calls=%fused_computation.19 | loop fusion | flops 824320 | bytes 3297312 | tf_op jit(solution)/shard_map/jit(_take)/select_n | solution.py:118
  49.6 1.1 copy-done.1
  50.7 8.4 %fusion.15 = f32[32,1,2,80,64]{4,0,2,3,1:T(8,128)} fusion(bf16[32,2,80,161]{3,2,1,0:T(8,128)(2,1)S(1)} %broadcast_select_fusion, f32[80,161,64,1]{1,0,2,3:T(8,128)S(1)} %bitcast.40), kind=kOutput, calls=%fused_computation.22 | convolution fusion | flops 633077760 | bytes 6256640 | tf_op jit(solution)/shard_map/fhrk,rkc->fhrc/dot_general | solution.py:97
  59.1 3.7 %copy.47 = f32[32,1,2,80,64]{3,4,2,1,0:T(8,128)} copy(f32[32,1,2,80,64]{4,0,2,3,1:T(8,128)} %fusion.15) | data formatting | bytes 2621440 | tf_op jit(solution)/shard_map/reshape | solution.py:9
  62.8 0.0 copy-start.3
  62.8 0.0 copy-start.2
  62.8 14.0 %all-to-all-start = ((f32[32,1,2,80,64]{3,4,2,1,0:T(8,128)}), f32[32,1,2,80,64]{3,4,2,1,0:T(8,128)}, u32[]{:S(2)}, u32[]{:S(2)}) async-start(f32[32,1,2,80,64]{3,4,2,1,0:T(8,128)} %copy.47), calls=%async_computation | async-start | bytes 4194304 | tf_op jit(solution)/shard_map/all_to_all | solution.py:14
  76.8 0.0 copy-done.3
  76.8 0.6 dynamic_slice.11
  78.7 0.0 copy-done.2
  78.7 0.6 dynamic_slice.9
  81.8 0.0 copy-done.4
  81.8 0.7 fusion.33
  83.2 0.0 copy-done.5
  83.2 0.7 fusion.32
  83.9 41.4 %all-to-all-done = f32[32,1,2,80,64]{3,4,2,1,0:T(8,128)} async-done(((f32[32,1,2,80,64]{3,4,2,1,0:T(8,128)}), f32[32,1,2,80,64]{3,4,2,1,0:T(8,128)}, u32[]{:S(2)}, u32[]{:S(2)}) %all-to-all-start) | async-done | bytes 1310752 | tf_op jit(solution)/shard_map/all_to_all | solution.py:14
  125.2 1.8 %reduce_sum.29 = f32[2,80,64]{1,2,0:T(8,128)S(1)} reduce(f32[32,1,2,80,64]{3,4,2,1,0:T(8,128)} %all-to-all-done, f32[]{:T(128)} %constant.108.clone.1), dimensions={0,1}, to_apply=%region_0.1 | reduce | flops 317440 | bytes 1351684 | tf_op jit(solution)/shard_map/reduce_sum | solution.py:15
  127.0 0.1 copy.57
  127.1 0.7 copy.49
  127.8 9.7 %all-to-all-start.1 = ((f32[1,2,80,64]{2,1,0,3:T(2,128)}), f32[1,2,80,64]{2,1,0,3:T(2,128)S(1)}, u32[]{:S(2)}, u32[]{:S(2)}) async-start(f32[1,2,80,64]{2,1,0,3:T(2,128)} %copy.49), calls=%async_computation.1 | async-start | bytes 131072 | tf_op jit(solution)/shard_map/all_to_all | solution.py:120
  137.5 1.3 fusion.28
  138.8 6.5 %all-to-all-done.1 = f32[1,2,80,64]{2,1,0,3:T(2,128)S(1)} async-done(((f32[1,2,80,64]{2,1,0,3:T(2,128)}), f32[1,2,80,64]{2,1,0,3:T(2,128)S(1)}, u32[]{:S(2)}, u32[]{:S(2)}) %all-to-all-start.1) | async-done | bytes 40992 | tf_op jit(solution)/shard_map/all_to_all | solution.py:120
  145.4 0.1 all_to_all.24
  145.5 4.8 %fusion.20 = f32[1,1,8,649]{3,2,1,0:T(8,128)S(1)} fusion(f32[1,1280,649]{1,0,2:T(1,128)} %param.13, f32[1,1280,1,4]{1,3,2,0:T(4,128)S(1)} %get-tuple-element.13, f32[1,1280,1,4]{1,3,2,0:T(4,128)S(1)} %get-tuple-element.12), kind=kOutput, calls=%fused_computation.23 | convolution fusion | flops 79759360 | bytes 3384608 | tf_op jit(solution)/shard_map/prc,frpq->fpqc/dot_general | solution.py:58
  150.2 0.1 fusion.31
  150.3 0.6 fusion.35
  151.6 0.7 pad_maximum_fusion.1
  152.3 0.6 broadcast_in_dim.73
  152.9 3.4 %all-to-all-start.2 = ((f32[16,1,2]{2,1,0:T(1,128)}), f32[16,1,2]{2,1,0:T(1,128)S(1)}, u32[]{:S(2)}, u32[]{:S(2)}) async-start(f32[16,1,2]{2,1,0:T(1,128)} %broadcast_in_dim.73), calls=%async_computation.2 | async-start | bytes 16384 | tf_op jit(solution)/shard_map/all_to_all | solution.py:20
  156.3 7.1 %all-to-all-done.2 = f32[16,1,2]{2,1,0:T(1,128)S(1)} async-done(((f32[16,1,2]{2,1,0:T(1,128)}), f32[16,1,2]{2,1,0:T(1,128)S(1)}, u32[]{:S(2)}, u32[]{:S(2)}) %all-to-all-start.2) | async-done | bytes 160 | tf_op jit(solution)/shard_map/all_to_all | solution.py:20
  163.4 0.6 fusion.36
  165.3 0.6 divide_multiply_fusion
  (10 shorter events, 0.1 us)
Async XLA Ops:
  0.0 45.2 %copy-start = (bf16[32,2,80,161]{3,2,1,0:T(8,128)(2,1)S(1)}, bf16[32,2,80,161]{3,2,1,0:T(8,128)(2,1)}, u32[]{:S(2)}) copy-start(bf16[32,2,80,161]{3,2,1,0:T(8,128)(2,1)} %param.7) | copy-start | bytes 4945924
  47.4 3.3 %copy-start.1 = (f32[80,161,32,2]{1,0,3,2:T(8,128)S(1)}, f32[80,161,32,2]{1,0,3,2:T(8,128)}, u32[]{:S(2)}) copy-start(f32[80,161,32,2]{1,0,3,2:T(8,128)} %copy.44) | copy-start | bytes 9891844
  62.8 14.0 %copy-start.3 = (s32[32]{0:T(128)S(1)}, s32[32]{0:T(128)}, u32[]{:S(2)}) copy-start(s32[32]{0:T(128)} %param.10) | copy-start | bytes 388
  62.8 15.9 %copy-start.2 = (s32[16]{0:T(128)S(1)}, s32[16]{0:T(128)}, u32[]{:S(2)}) copy-start(s32[16]{0:T(128)} %param.9) | copy-start | bytes 196
  62.8 19.1 %copy-start.4 = (s32[4]{0:T(128)S(1)}, s32[4]{0:T(128)}, u32[]{:S(2)}) copy-start(s32[4]{0:T(128)} %param.11) | copy-start | bytes 52
  62.8 20.4 %copy-start.5 = (f32[4]{0:T(128)S(1)}, f32[4]{0:T(128)}, u32[]{:S(2)}) copy-start(f32[4]{0:T(128)} %param.12) | copy-start | bytes 52
  62.8 62.5 %all-to-all-start = ((f32[32,1,2,80,64]{3,4,2,1,0:T(8,128)}), f32[32,1,2,80,64]{3,4,2,1,0:T(8,128)}, u32[]{:S(2)}, u32[]{:S(2)}) async-start(f32[32,1,2,80,64]{3,4,2,1,0:T(8,128)} %copy.47), calls=%async_computation | async-start | bytes 4194304 | tf_op jit(solution)/shard_map/all_to_all | solution.py:14
  127.8 17.6 %all-to-all-start.1 = ((f32[1,2,80,64]{2,1,0,3:T(2,128)}), f32[1,2,80,64]{2,1,0,3:T(2,128)S(1)}, u32[]{:S(2)}, u32[]{:S(2)}) async-start(f32[1,2,80,64]{2,1,0,3:T(2,128)} %copy.49), calls=%async_computation.1 | async-start | bytes 131072 | tf_op jit(solution)/shard_map/all_to_all | solution.py:120
  152.9 10.5 %all-to-all-start.2 = ((f32[16,1,2]{2,1,0:T(1,128)}), f32[16,1,2]{2,1,0:T(1,128)S(1)}, u32[]{:S(2)}, u32[]{:S(2)}) async-start(f32[16,1,2]{2,1,0:T(1,128)} %broadcast_in_dim.73), calls=%async_computation.2 | async-start | bytes 16384 | tf_op jit(solution)/shard_map/all_to_all | solution.py:20
where the time goes:
time: 166 us
  waiting for transfers between devices  55 us (33%)
  other arithmetic  48.3 us (29%)
  starting transfers between devices  27.1 us (16%)
  local copies, waits for them, and re-layouts  15.9 us (10%)
  matrix products  13.1 us (8%)
  between operations  6.53 us (4%)
    all_to_all x1, waiting for transfers between devices, sum_at_owner(): tiles = lax.all_to_all(in_blocks(shard, dim, size), axis, 0, 0, tiled=True)  41.4 us
    mul x1, other arithmetic, cycle_table(): jnp.cos(angles) * factor  34.9 us
    all_to_all x1, starting transfers between devices, sum_at_owner(): tiles = lax.all_to_all(in_blocks(shard, dim, size), axis, 0, 0, tiled=True)  14 us
    all_to_all x1, starting transfers between devices, shards(): lax.all_to_all(summed, 'ns', split_axis=3, concat_axis=2, tiled=True)  9.75 us
    dot_general x1, matrix products, segment_terms_of(): jnp.einsum('fhrk,rkc->fhrc', picked_rows.astype(jnp.float32), trig_values...  8.38 us
    all_to_all x1, waiting for transfers between devices, sent_to_all(): lax.all_to_all(jnp.broadcast_to(shard[None], (size, *shard.shape)), axis,...  7.07 us
    all_to_all x1, waiting for transfers between devices, shards(): lax.all_to_all(summed, 'ns', split_axis=3, concat_axis=2, tiled=True)  6.53 us
    another operation x1, local copies, waits for them, and re-layouts, cycle_table(): jnp.stack([jnp.cos(angles) * factor, -jnp.sin(angles) * factor], -1)  5.34 us
  transfers between devices with their start and end apart: 3, of which 3 were waited for; matrix products, arithmetic and copies ran while one was open for 2% of the time, Pallas kernels for 0%

commit v1 on v0

v1 whole, which is shorter than its diff:
```python
import functools

import jax
import jax.numpy as jnp
import numpy as np
from jax import lax
from jax.experimental import pallas as pl
from jax.experimental.pallas import tpu as pltpu
from jax.sharding import PartitionSpec as P

MESH = pl.DeviceIdType.MESH
NX = 4
NZ = 8
NS = 16
CH = 16
F32 = jnp.float32
BF16 = jnp.bfloat16


def _fit(function, terms):
    z = 0.125 + 0.125 * np.cos(np.pi * (np.arange(200) + 0.5) / 200)
    cheb = np.polynomial.chebyshev.Chebyshev.fit(z, function(np.sqrt(z)), terms - 1, domain=[0, 0.25])
    return [float(v) for v in cheb.convert(kind=np.polynomial.Polynomial).coef]


COS = _fit(lambda t: np.cos(2 * np.pi * t), 8)
SIN = _fit(lambda t: np.sin(2 * np.pi * t) / t, 8)


def _horner(coefs, z):
    total = jnp.full_like(z, coefs[-1])
    for c in coefs[-2::-1]:
        total = total * z + c
    return total


def _cos_sin(product, length, inverse):
    rest = product - jnp.round(product * inverse) * length
    t = rest * inverse
    z = t * t
    return _horner(COS, z), t * _horner(SIN, z)


def kernel(
    truncation, levels,
    band_s, waves_s, order_s, bits_s, power_s, grid_hbm, leg_hbm,
    out_ref,
    gridv, legv, leghi, leglo, xf, w, cs, sbuf, rx, zbuf, rz, obuf, ybuf, ry, rmm,
    grid_sem, leg_sem, xs_sem, xr_sem, zs_sem, zr_sem, ys_sem, yr_sem, ms_sem, mr_sem,
):
    ew, ns = lax.axis_index("ew"), lax.axis_index("ns")
    x, z = lax.rem(ew, NX), lax.div(ew, NX)
    rows = gridv.shape[2]
    points = gridv.shape[3]
    chunks = rows // CH

    grid_copy = pltpu.make_async_copy(grid_hbm, gridv, grid_sem)
    grid_copy.start()
    leg_copy = pltpu.make_async_copy(leg_hbm, legv, leg_sem)
    leg_copy.start()

    barrier = pltpu.get_barrier_semaphore()
    for d in range(1, NX):
        pl.semaphore_signal(barrier, inc=1, device_id={"ew": z * NX + lax.rem(x + d, NX)}, device_id_type=MESH)
    for d in range(1, NZ):
        pl.semaphore_signal(barrier, inc=1, device_id={"ew": lax.rem(z + d, NZ) * NX + x}, device_id_type=MESH)
    for d in range(1, NS):
        pl.semaphore_signal(barrier, inc=1, device_id={"ns": lax.rem(ns + d, NS)}, device_id_type=MESH)

    w[...] = jnp.zeros_like(w)
    xf[...] = jnp.zeros_like(xf)

    lane = lax.broadcasted_iota(jnp.int32, (16, 128), 1)
    sub16 = lax.broadcasted_iota(jnp.int32, (16, 128), 0)
    pair_of = (lane & 63) >> 2
    wave = jnp.zeros((16, 128), jnp.int32)
    for p in range(16):
        wave = jnp.where(pair_of == p, waves_s[p], wave)
    wave = jnp.where((lane & 2) == 0, wave, truncation - wave).astype(F32)
    imaginary = (lane & 1) == 1
    low_half = lane < 64
    first = ew * points
    product_a = wave * (first + 16 * sub16).astype(F32)
    product_b = wave * sub16.astype(F32)
    point0 = (first + sub16).astype(F32)
    point_end = (first + points).astype(F32)

    grid_copy.wait()

    def chunk(c, _):
        def convert(zz, _):
            for xx in range(NX):
                field = order_s[zz * NX + xx]
                for h in range(2):
                    at = pl.multiple_of((h * 32 + xx * NZ + zz) * CH, CH)
                    block = gridv[field, h, pl.ds(pl.multiple_of(c * CH, CH), CH), :].astype(F32)
                    xf[0, pl.ds(at, CH), :] = block[:, 0:128]
                    xf[1, pl.ds(at, CH), 0 : points - 128] = block[:, 128:points]
            return 0

        lax.fori_loop(0, NZ, convert, 0)

        def half(g, _):
            for j in range(4):
                row0 = g * 8 + j
                band0 = band_s[ns * rows + c * CH + row0]
                band1 = band_s[ns * rows + c * CH + row0 + 4]
                length = jnp.where(low_half, 20 + 4 * band0, 20 + 4 * band1).astype(F32)
                inverse = 1.0 / length
                cos_a, sin_a = _cos_sin(product_a, length, inverse)
                cos_b, sin_b = _cos_sin(product_b, length, inverse)
                cs[j, 0] = jnp.where(imaginary, -sin_a, cos_a) * inverse
                cs[j, 1] = jnp.where(imaginary, cos_a, sin_a) * inverse
                end = jnp.minimum(length, point_end) - point0
                for a in range(11):
                    value = cs[j, 0, a : a + 1, :] * cos_b - cs[j, 1, a : a + 1, :] * sin_b
                    value = jnp.where(end > 16.0 * a, value, 0.0)
                    high = value.astype(BF16)
                    low = (value - high.astype(F32)).astype(BF16)
                    w[j, 16 * a : 16 * a + 16, 0:128] = high
                    w[j, 16 * a : 16 * a + 16, 128:256] = low
                sides = []
                for side in range(2):
                    x0 = xf[side, pl.ds(row0, 64, stride=CH), :].astype(BF16)
                    x1 = xf[side, pl.ds(row0 + 4, 64, stride=CH), :].astype(BF16)
                    sides.append(jnp.concatenate([x0, x1], 0))
                both = jnp.dot(jnp.concatenate(sides, 1), w[j], preferred_element_type=F32)
                both = both[:, :128] + both[:, 128:]
                out = jnp.where(lax.broadcasted_iota(jnp.int32, (64, 128), 1) < 64, both[:64], both[64:])
                for h in range(2):
                    for xx in range(NX):
                        sbuf[c, xx, pl.ds(g * 8 + h * 4 + j, NZ, stride=CH), :] = out[h * 32 + xx * NZ : h * 32 + xx * NZ + NZ]
            return 0

        lax.fori_loop(0, CH // 8, half, 0)

        @pl.when(c == 0)
        def _():
            pl.semaphore_wait(barrier, NX - 1 + NZ - 1 + NS - 1)

        for d in range(1, NX):
            x_copy(c, d).start()
        return 0

    def x_copy(c, d):
        to = lax.rem(x + d, NX)
        return pltpu.make_async_remote_copy(
            src_ref=sbuf.at[c, to], dst_ref=rx.at[c, d - 1],
            send_sem=xs_sem.at[c, d - 1], recv_sem=xr_sem.at[c, d - 1],
            device_id={"ew": z * NX + to}, device_id_type=MESH)

    def z_copy(c, d):
        to = lax.rem(z + d, NZ)
        return pltpu.make_async_remote_copy(
            src_ref=zbuf.at[c, pl.ds(pl.multiple_of(to * CH, CH), CH)], dst_ref=rz.at[c, d - 1],
            send_sem=zs_sem.at[c, d - 1], recv_sem=zr_sem.at[c, d - 1],
            device_id={"ew": to * NX + x}, device_id_type=MESH)

    def y_copy(d):
        to = lax.rem(ns + d, NS)
        return pltpu.make_async_remote_copy(
            src_ref=ybuf.at[to], dst_ref=ry.at[ns],
            send_sem=ys_sem.at[d - 1], recv_sem=yr_sem.at[d - 1],
            device_id={"ns": to}, device_id_type=MESH)

    def m_copy(d):
        to = lax.rem(ns + d, NS)
        return pltpu.make_async_remote_copy(
            src_ref=rmm.at[0], dst_ref=rmm.at[d],
            send_sem=ms_sem.at[d - 1], recv_sem=mr_sem.at[d - 1],
            device_id={"ns": to}, device_id_type=MESH)

    lax.fori_loop(0, chunks, chunk, 0)

    leg_copy.wait()

    def split(i, _):
        at = pl.ds(pl.multiple_of(i * 80, 16), 80)
        value = legv[at, :]
        high = value.astype(BF16)
        leghi[at, :] = high
        leglo[at, :] = (value - high.astype(F32)).astype(BF16)
        return 0

    lax.fori_loop(0, legv.shape[0] // 80, split, 0)

    def second(c, _):
        for d in range(1, NX):
            x_copy(c, d).wait_recv()
        zbuf[c] = sbuf[c, x] + rx[c, 0] + rx[c, 1] + rx[c, 2]
        for d in range(1, NZ):
            z_copy(c, d).start()
        return 0

    lax.fori_loop(0, chunks, second, 0)

    sub8 = lax.broadcasted_iota(jnp.int32, (8, 128), 0)
    lane8 = lax.broadcasted_iota(jnp.int32, (8, 128), 1)
    obuf[...] = jnp.zeros_like(obuf)

    def third(c, _):
        for d in range(1, NZ):
            z_copy(c, d).wait_recv()
        total = zbuf[c, pl.ds(pl.multiple_of(z * CH, CH), CH)]
        for d in range(NZ - 1):
            total = total + rz[c, d]
        for g in range(CH // 8):
            o = total[g * 8 : g * 8 + 8]
            r = pltpu.roll(o, 4, 0)
            o = jnp.where(sub8 < 4, o + r, r - o)
            r = pltpu.roll(pltpu.roll(o, 4, 0), 64, 1)
            o = jnp.where((sub8 < 4) == (lane8 < 64), o, r)
            obuf[pl.ds(pl.multiple_of(c * CH + g * 8, 8), 8), :] = o
        return 0

    lax.fori_loop(0, chunks, third, 0)

    turned = obuf[...].T
    for p in range(NS):
        ybuf[p] = jnp.concatenate([turned[4 * p : 4 * p + 4], turned[64 + 4 * p : 68 + 4 * p]], 0)
    for d in range(1, NS):
        y_copy(d).start()
    ry[ns] = ybuf[ns]

    columns = legv.shape[1]
    column = lax.broadcasted_iota(jnp.int32, (2, columns), 1)
    wavenum = waves_s[ns]
    in_first = column <= truncation - wavenum
    shifted = jnp.where(in_first, column, column - (truncation - wavenum + 1))
    even = (shifted & 1) == 0
    degree = jnp.where(in_first, wavenum + column, column - 1).astype(F32)
    field_type = lax.div(order_s[ew], levels)
    power, bits = power_s[0], bits_s[0]
    for t in range(1, bits_s.shape[0]):
        power = jnp.where(field_type == t, power_s[t], power)
        bits = jnp.where(field_type == t, bits_s[t], bits)
    weight = jnp.exp(power * jnp.log(degree * (degree + 1.0) + 2.0))
    spread = (lax.shift_left(jnp.int32(1), bits) - 1).astype(F32) * (1.0 / 4096.0)

    for d in range(1, NS):
        y_copy(d).wait_recv()
    pieces = [None] * (rows * NS // 128)
    for i in range(NS):
        at, off = divmod(i * rows, 128)
        value = ry[i] if off == 0 else pltpu.roll(ry[i], off, 1)
        if off + rows <= 128:
            parts = [(at, value)]
        else:
            parts = [(at, jnp.where(lane8 >= off, value, 0.0)), (at + 1, jnp.where(lane8 < off, value, 0.0))]
        for k, v in parts:
            pieces[k] = v if pieces[k] is None else pieces[k] + v
    stacked = jnp.concatenate(pieces, 1)
    high = stacked.astype(BF16).astype(F32)
    both = jnp.concatenate([high, stacked - high], 0).astype(BF16)
    by_high = jnp.dot(both, leghi[...], preferred_element_type=F32)
    by_low = jnp.dot(both, leglo[...], preferred_element_type=F32)
    result = by_high[:8] + by_high[8:] + by_low[:8]

    chosen = jnp.where(
        in_first,
        jnp.where(even, result[0:2], result[4:6]),
        jnp.where(even, result[2:4], result[6:8]),
    )
    scaled = chosen * weight
    most = jnp.max(scaled)
    least = jnp.min(scaled)
    rmm[0] = jnp.where(lane8 < 64, most, -least)
    for d in range(1, NS):
        m_copy(d).start()
    for d in range(1, NS):
        m_copy(d).wait_recv()
    top = rmm[0]
    for d in range(1, NS):
        top = jnp.maximum(top, rmm[d])
    highest = jnp.max(jnp.where(lane8 < 64, top, -jnp.inf))
    lowest = -jnp.max(jnp.where(lane8 < 64, -jnp.inf, top))
    span = highest - lowest + 1e-6
    out_ref[0, 0] = (scaled - lowest) / span * spread

    def sent(c, _):
        for d in range(1, NX):
            x_copy(c, d).wait_send()
        for d in range(1, NZ):
            z_copy(c, d).wait_send()
        return 0

    lax.fori_loop(0, chunks, sent, 0)
    for d in range(1, NS):
        y_copy(d).wait_send()
        m_copy(d).wait_send()


def shards(grid, band_rows, wave_pairs, packer_order, field_bits, field_power, legendre):
    fields, hemis, rows, points = grid.shape
    lats, columns = legendre.shape[1:]
    truncation = columns - 2
    levels = fields // field_bits.shape[0]
    chunks = rows // CH
    smem = pl.BlockSpec(memory_space=pltpu.SMEM)
    hbm = pl.BlockSpec(memory_space=pl.ANY)
    dma = pltpu.SemaphoreType.DMA
    return pl.pallas_call(
        functools.partial(kernel, truncation, levels),
        out_shape=jax.ShapeDtypeStruct((1, 1, 2, columns), F32),
        in_specs=[smem] * 5 + [hbm] * 2,
        out_specs=pl.BlockSpec(memory_space=pltpu.VMEM),
        scratch_shapes=[
            pltpu.VMEM((fields, hemis, rows, points), BF16),
            pltpu.VMEM((lats, columns), F32),
            pltpu.VMEM((lats, columns), BF16),
            pltpu.VMEM((lats, columns), BF16),
            pltpu.VMEM((2, fields * hemis * CH, 128), F32),
            pltpu.VMEM((4, 256, 256), BF16),
            pltpu.VMEM((4, 2, 16, 128), F32),
            pltpu.VMEM((chunks, NX, NZ * CH, 128), F32),
            pltpu.VMEM((chunks, NX - 1, NZ * CH, 128), F32),
            pltpu.VMEM((chunks, NZ * CH, 128), F32),
            pltpu.VMEM((chunks, NZ - 1, CH, 128), F32),
            pltpu.VMEM((128, 128), F32),
            pltpu.VMEM((NS, 8, 128), F32),
            pltpu.VMEM((NS, 8, 128), F32),
            pltpu.VMEM((NS, 8, 128), F32),
            dma,
            dma,
            dma((chunks, NX - 1)),
            dma((chunks, NX - 1)),
            dma((chunks, NZ - 1)),
            dma((chunks, NZ - 1)),
            dma((NS - 1,)),
            dma((NS - 1,)),
            dma((NS - 1,)),
            dma((NS - 1,)),
        ],
        compiler_params=pltpu.CompilerParams(
            collective_id=0, has_side_effects=True, vmem_limit_bytes=48 * 2**20
        ),
    )(band_rows, wave_pairs, packer_order, field_bits, field_power, grid, legendre.reshape(lats, columns))


def solution(mesh):
    return jax.shard_map(
        shards,
        mesh=mesh,
        in_specs=(P(None, None, "ns", "ew"), P(), P(), P(), P(), P(), P("ns", None, None)),
        out_specs=P("ew", "ns", None, None),
        check_vma=False,
    )
```

time: 166 us -> 60 us (0.36)
  waiting for transfers between devices: 55 us -> 0 us
  Pallas kernels: 0 us -> 51.1 us
  other arithmetic: 48.3 us -> 0 us
  starting transfers between devices: 27.1 us -> 0 us
  matrix products: 13.1 us -> 0 us
  local copies, waits for them, and re-layouts: 15.9 us -> 8.58 us
  between operations: 6.53 us -> 0.07 us
    all_to_all x3 -> x0, waiting for transfers between devices: 55 us -> none  [the longest x1 41.4 us: sum_at_owner(): tiles = lax.all_to_all(in_blocks(shard, dim, size), axis, 0, 0, tiled=True)]
    pallas_call x0 -> x1, Pallas kernels: none -> 51.1 us  [shards(): pl.pallas_call(functools.partial(kernel, truncation, levels), out_shape=j...]
    mul x3 -> x0, other arithmetic: 35.6 us -> none  [the longest x1 34.9 us: cycle_table(): jnp.cos(angles) * factor]
    all_to_all x3 -> x0, starting transfers between devices: 27.1 us -> none  [the longest x1 14 us: sum_at_owner(): tiles = lax.all_to_all(in_blocks(shard, dim, size), axis, 0, 0, tiled=True)]
    dot_general x2 -> x0, matrix products: 13.1 us -> none  [the longest x1 8.38 us: segment_terms_of(): jnp.einsum('fhrk,rkc->fhrc', picked_rows.astype(jnp.float32), trig_values...]
    unnamed x13 -> x14, local copies, waits for them, and re-layouts: 1.2 us -> 8.58 us
    another operation x2 -> x0, local copies, waits for them, and re-layouts: 5.43 us -> none  [the longest x1 5.34 us: cycle_table(): jnp.stack([jnp.cos(angles) * factor, -jnp.sin(angles) * factor], -1)]
    reshape x1 -> x0, local copies, waits for them, and re-layouts: 3.69 us -> none  [in_blocks(): return jnp.moveaxis(shard.reshape(*before, size, -1, *after), dim, 0)]
  transfers between devices with their start and end apart: 3 -> 0, of which waited for: 3 -> 0; matrix products, arithmetic and copies ran while one was open for 2% -> 0% of each run, Pallas kernels for 0% -> 0%
where the time goes in v1:
time: 60 us; the launch traced here: 59.8 us
  Pallas kernels  51.1 us (85%)
  local copies, waits for them, and re-layouts  8.58 us (14%)
    pallas_call x1, Pallas kernels, shards(): pl.pallas_call(functools.partial(kernel, truncation, levels), out_shape=j...  51.1 us
    unnamed x14, local copies, waits for them, and re-layouts  8.58 us

profile of v1, /device:TPU:1, one launch (start us, length us, event | category | flops | bytes accessed | tf_op | source)
XLA Modules:
  0.0 59.8 jit_solution(16587024847309596105)
XLA Ops:
  0.0 0.0 copy-start.5
  0.0 0.0 copy-start.4
  0.0 0.0 copy-start.3
  0.0 0.0 copy-start.2
  0.0 0.0 copy-start.1
  0.0 0.0 copy-start
  0.0 8.0 %copy.8 = f32[1,1280,649]{2,1,0:T(8,128)} copy(f32[1,1280,649]{1,0,2:T(1,128)} %param.13) | data formatting | bytes 6645760 | tf_op args[6]
  8.0 0.0 copy-done.5
  8.0 0.0 copy-done.4
  8.0 0.0 copy-done.3
  8.0 0.0 copy-done.2
  8.0 0.0 copy-done.1
  8.0 0.0 copy-done
  8.0 51.1 %shard_map.73 = f32[1,1,2,649]{3,2,1,0:T(2,128)S(1)} custom-call(s32[1280]{0:T(1024)S(1)} %copy-done.1, s32[16]{0:T(128)S(1)} %copy-done.2, s32[32]{0:T(128)S(1)} %copy-done.3, s32[4]{0:T(128)S(1)} %copy-done.4, f32[4]{0:T(128)S(1)} %copy-done.5, bf16[32,2,80,161]{3,2,1,0:T(8,128)(2,1)S(1)} %copy-done, f32[1280,649]{1,0:T(8,128)} %bitcast.1), custom_call_target="tpu_custom_call" | custom-call | tf_op jit(solution)/shard_map/pallas_call | solution.py:302
  59.2 0.6 copy.10
Async XLA Ops:
  0.0 8.0 %copy-start.5 = (f32[4]{0:T(128)S(1)}, f32[4]{0:T(128)}, u32[]{:S(2)}) copy-start(f32[4]{0:T(128)} %power_s.1) | copy-start | bytes 52
  0.0 8.0 %copy-start.4 = (s32[4]{0:T(128)S(1)}, s32[4]{0:T(128)}, u32[]{:S(2)}) copy-start(s32[4]{0:T(128)} %bits_s.1) | copy-start | bytes 52
  0.0 8.0 %copy-start.3 = (s32[32]{0:T(128)S(1)}, s32[32]{0:T(128)}, u32[]{:S(2)}) copy-start(s32[32]{0:T(128)} %order_s.1) | copy-start | bytes 388
  0.0 8.0 %copy-start.2 = (s32[16]{0:T(128)S(1)}, s32[16]{0:T(128)}, u32[]{:S(2)}) copy-start(s32[16]{0:T(128)} %waves_s.1) | copy-start | bytes 196
  0.0 8.0 %copy-start.1 = (s32[1280]{0:T(1024)S(1)}, s32[1280]{0:T(1024)}, u32[]{:S(2)}) copy-start(s32[1280]{0:T(1024)} %band_s.1) | copy-start | bytes 15364
  0.0 8.0 %copy-start = (bf16[32,2,80,161]{3,2,1,0:T(8,128)(2,1)S(1)}, bf16[32,2,80,161]{3,2,1,0:T(8,128)(2,1)}, u32[]{:S(2)}) copy-start(bf16[32,2,80,161]{3,2,1,0:T(8,128)(2,1)} %grid_hbm.1) | copy-start | bytes 4945924

commit v2 on v1

--- a/solution.py
+++ b/solution.py
@@ -56,8 +56,12 @@
 
     grid_copy = pltpu.make_async_copy(grid_hbm, gridv, grid_sem)
     grid_copy.start()
-    leg_copy = pltpu.make_async_copy(leg_hbm, legv, leg_sem)
-    leg_copy.start()
+    leg_copies = [
+        pltpu.make_async_copy(leg_hbm.at[:, 0, k * 128 : (k + 1) * 128], legv.at[k], leg_sem.at[k])
+        for k in range(legv.shape[0])
+    ]
+    for copy in leg_copies:
+        copy.start()
 
     barrier = pltpu.get_barrier_semaphore()
     for d in range(1, NX):
@@ -172,17 +176,18 @@
 
     lax.fori_loop(0, chunks, chunk, 0)
 
-    leg_copy.wait()
+    for copy in leg_copies:
+        copy.wait()
 
     def split(i, _):
-        at = pl.ds(pl.multiple_of(i * 80, 16), 80)
-        value = legv[at, :]
+        at = pl.ds(pl.multiple_of(i * 128, 128), 128)
+        value = legv[i].T
         high = value.astype(BF16)
         leghi[at, :] = high
         leglo[at, :] = (value - high.astype(F32)).astype(BF16)
         return 0
 
-    lax.fori_loop(0, legv.shape[0] // 80, split, 0)
+    lax.fori_loop(0, legv.shape[0], split, 0)
 
     def second(c, _):
         for d in range(1, NX):
@@ -222,7 +227,7 @@
         y_copy(d).start()
     ry[ns] = ybuf[ns]
 
-    columns = legv.shape[1]
+    columns = leghi.shape[1]
     column = lax.broadcasted_iota(jnp.int32, (2, columns), 1)
     wavenum = waves_s[ns]
     in_first = column <= truncation - wavenum
@@ -297,7 +302,7 @@
     levels = fields // field_bits.shape[0]
     chunks = rows // CH
     smem = pl.BlockSpec(memory_space=pltpu.SMEM)
-    hbm = pl.BlockSpec(memory_space=pl.ANY)
+    hbm = pl.BlockSpec(memory_space=pltpu.HBM)
     dma = pltpu.SemaphoreType.DMA
     return pl.pallas_call(
         functools.partial(kernel, truncation, levels),
@@ -306,7 +311,7 @@
         out_specs=pl.BlockSpec(memory_space=pltpu.VMEM),
         scratch_shapes=[
             pltpu.VMEM((fields, hemis, rows, points), BF16),
-            pltpu.VMEM((lats, columns), F32),
+            pltpu.VMEM((lats // 128, columns, 128), F32),
             pltpu.VMEM((lats, columns), BF16),
             pltpu.VMEM((lats, columns), BF16),
             pltpu.VMEM((2, fields * hemis * CH, 128), F32),
@@ -321,7 +326,7 @@
             pltpu.VMEM((NS, 8, 128), F32),
             pltpu.VMEM((NS, 8, 128), F32),
             dma,
-            dma,
+            dma((lats // 128,)),
             dma((chunks, NX - 1)),
             dma((chunks, NX - 1)),
             dma((chunks, NZ - 1)),
@@ -332,9 +337,9 @@
             dma((NS - 1,)),
         ],
         compiler_params=pltpu.CompilerParams(
-            collective_id=0, has_side_effects=True, vmem_limit_bytes=48 * 2**20
+            collective_id=0, has_side_effects=True, vmem_limit_bytes=61 * 2**20
         ),
-    )(band_rows, wave_pairs, packer_order, field_bits, field_power, grid, legendre.reshape(lats, columns))
+    )(band_rows, wave_pairs, packer_order, field_bits, field_power, grid, jnp.transpose(legendre, (2, 0, 1)))
 
 
 def solution(mesh):

time: 60 us -> 52.4 us (0.87)
  local copies, waits for them, and re-layouts: 8.58 us -> 1.29 us
    unnamed x14 -> x1, local copies, waits for them, and re-layouts: 8.58 us -> 1.29 us
where the time goes in v2:
time: 52.4 us; the launch traced here: 52.2 us
  Pallas kernels  50.9 us (97%)
  local copies, waits for them, and re-layouts  1.29 us (2%)
    pallas_call x1, Pallas kernels, shards(): pl.pallas_call(functools.partial(kernel, truncation, levels), out_shape=j...  50.9 us
    unnamed x1, local copies, waits for them, and re-layouts  1.29 us

profile of v2, /device:TPU:1, one launch (start us, length us, event | category | flops | bytes accessed | tf_op | source)
XLA Modules:
  0.0 52.2 jit_solution(18050414350358673921)
XLA Ops:
  0.0 50.9 %shard_map.73 = f32[1,1,2,649]{3,2,1,0:T(2,128)} custom-call(s32[1280]{0:T(1024)} %band_s.1, s32[16]{0:T(128)} %waves_s.1, s32[32]{0:T(128)} %order_s.1, s32[4]{0:T(128)} %bits_s.1, f32[4]{0:T(128)} %power_s.1, bf16[32,2,80,161]{3,2,1,0:T(8,128)(2,1)} %grid_hbm.1, f32[649,1,1280]{2,1,0:T(1,128)} %bitcast.1), custom_call_target="tpu_custom_call" | custom-call | tf_op jit(solution)/shard_map/pallas_call | solution.py:307
  50.9 1.3 %copy.9 = f32[1,1,2,649]{3,2,1,0:T(2,128)} copy(f32[1,1,2,649]{3,2,1,0:T(2,128)} %shard_map.73) | data formatting | bytes 10384

commit v3 on v2

--- a/solution.py
+++ b/solution.py
@@ -13,6 +13,7 @@
 NZ = 8
 NS = 16
 CH = 16
+HALF = NZ * CH // 2
 F32 = jnp.float32
 BF16 = jnp.bfloat16
 
@@ -45,8 +46,8 @@
     truncation, levels,
     band_s, waves_s, order_s, bits_s, power_s, grid_hbm, leg_hbm,
     out_ref,
-    gridv, legv, leghi, leglo, xf, w, cs, sbuf, rx, zbuf, rz, obuf, ybuf, ry, rmm,
-    grid_sem, leg_sem, xs_sem, xr_sem, zs_sem, zr_sem, ys_sem, yr_sem, ms_sem, mr_sem,
+    gridv, legv, leghi, leglo, xf, w, cs, sbuf, rfar, rx, zbuf, rz, obuf, ybuf, ry, rmm,
+    grid_sem, leg_sem, fs_sem, fr_sem, xs_sem, xr_sem, zs_sem, zr_sem, ys_sem, yr_sem, ms_sem, mr_sem,
 ):
     ew, ns = lax.axis_index("ew"), lax.axis_index("ns")
     x, z = lax.rem(ew, NX), lax.div(ew, NX)
@@ -72,7 +73,7 @@
         pl.semaphore_signal(barrier, inc=1, device_id={"ns": lax.rem(ns + d, NS)}, device_id_type=MESH)
 
     w[...] = jnp.zeros_like(w)
-    xf[...] = jnp.zeros_like(xf)
+    xf[1] = jnp.zeros_like(xf[1])
 
     lane = lax.broadcasted_iota(jnp.int32, (16, 128), 1)
     sub16 = lax.broadcasted_iota(jnp.int32, (16, 128), 0)
@@ -90,6 +91,58 @@
     point_end = (first + points).astype(F32)
 
     grid_copy.wait()
+
+    def neighbour(side):
+        return lax.rem(x + (1 if side == 0 else NX - 1), NX)
+
+    def far_copy(c, side):
+        return pltpu.make_async_remote_copy(
+            src_ref=sbuf.at[c, lax.rem(x + 2, NX), pl.ds(side * HALF, HALF)], dst_ref=rfar.at[c, side],
+            send_sem=fs_sem.at[c, side], recv_sem=fr_sem.at[c, side],
+            device_id={"ew": z * NX + neighbour(side)}, device_id_type=MESH)
+
+    def near_copy(c, side, part):
+        rows = pl.ds(part * HALF, HALF)
+        return pltpu.make_async_remote_copy(
+            src_ref=sbuf.at[c, neighbour(side), rows], dst_ref=rx.at[c, side, rows],
+            send_sem=xs_sem.at[c, side, part], recv_sem=xr_sem.at[c, side, part],
+            device_id={"ew": z * NX + neighbour(side)}, device_id_type=MESH)
+
+    def z_copy(c, d):
+        to = lax.rem(z + d, NZ)
+        return pltpu.make_async_remote_copy(
+            src_ref=zbuf.at[c, pl.ds(pl.multiple_of(to * CH, CH), CH)], dst_ref=rz.at[c, d - 1],
+            send_sem=zs_sem.at[c, d - 1], recv_sem=zr_sem.at[c, d - 1],
+            device_id={"ew": to * NX + x}, device_id_type=MESH)
+
+    def y_copy(d):
+        to = lax.rem(ns + d, NS)
+        return pltpu.make_async_remote_copy(
+            src_ref=ybuf.at[to], dst_ref=ry.at[ns],
+            send_sem=ys_sem.at[d - 1], recv_sem=yr_sem.at[d - 1],
+            device_id={"ns": to}, device_id_type=MESH)
+
+    def m_copy(d):
+        to = lax.rem(ns + d, NS)
+        return pltpu.make_async_remote_copy(
+            src_ref=rmm.at[0, 0:1], dst_ref=rmm.at[d, 0:1],
+            send_sem=ms_sem.at[d - 1], recv_sem=mr_sem.at[d - 1],
+            device_id={"ns": to}, device_id_type=MESH)
+
+    def pass_on(c):
+        for side in (0, 1):
+            far_copy(c, side).wait_recv()
+            rows = pl.ds(side * HALF, HALF)
+            sbuf[c, neighbour(side), rows] = sbuf[c, neighbour(side), rows] + rfar[c, side]
+            near_copy(c, side, side).start()
+
+    def along_z(c):
+        for side in (0, 1):
+            for part in (0, 1):
+                near_copy(c, side, part).wait_recv()
+        zbuf[c] = sbuf[c, x] + rx[c, 0] + rx[c, 1]
+        for d in range(1, NZ):
+            z_copy(c, d).start()
 
     def chunk(c, _):
         def convert(zz, _):
@@ -142,39 +195,27 @@
         def _():
             pl.semaphore_wait(barrier, NX - 1 + NZ - 1 + NS - 1)
 
-        for d in range(1, NX):
-            x_copy(c, d).start()
-        return 0
-
-    def x_copy(c, d):
-        to = lax.rem(x + d, NX)
-        return pltpu.make_async_remote_copy(
-            src_ref=sbuf.at[c, to], dst_ref=rx.at[c, d - 1],
-            send_sem=xs_sem.at[c, d - 1], recv_sem=xr_sem.at[c, d - 1],
-            device_id={"ew": z * NX + to}, device_id_type=MESH)
-
-    def z_copy(c, d):
-        to = lax.rem(z + d, NZ)
-        return pltpu.make_async_remote_copy(
-            src_ref=zbuf.at[c, pl.ds(pl.multiple_of(to * CH, CH), CH)], dst_ref=rz.at[c, d - 1],
-            send_sem=zs_sem.at[c, d - 1], recv_sem=zr_sem.at[c, d - 1],
-            device_id={"ew": to * NX + x}, device_id_type=MESH)
-
-    def y_copy(d):
-        to = lax.rem(ns + d, NS)
-        return pltpu.make_async_remote_copy(
-            src_ref=ybuf.at[to], dst_ref=ry.at[ns],
-            send_sem=ys_sem.at[d - 1], recv_sem=yr_sem.at[d - 1],
-            device_id={"ns": to}, device_id_type=MESH)
-
-    def m_copy(d):
-        to = lax.rem(ns + d, NS)
-        return pltpu.make_async_remote_copy(
-            src_ref=rmm.at[0], dst_ref=rmm.at[d],
-            send_sem=ms_sem.at[d - 1], recv_sem=mr_sem.at[d - 1],
-            device_id={"ns": to}, device_id_type=MESH)
+        for side in (0, 1):
+            far_copy(c, side).start()
+            near_copy(c, side, 1 - side).start()
+
+        @pl.when(c >= 2)
+        def _():
+            pass_on(c - 2)
+
+        return 0
 
     lax.fori_loop(0, chunks, chunk, 0)
+
+    pass_on(chunks - 2)
+    along_z(0)
+    pass_on(chunks - 1)
+
+    def second(c, _):
+        along_z(c)
+        return 0
+
+    lax.fori_loop(1, chunks, second, 0)
 
     for copy in leg_copies:
         copy.wait()
@@ -188,16 +229,6 @@
         return 0
 
     lax.fori_loop(0, legv.shape[0], split, 0)
-
-    def second(c, _):
-        for d in range(1, NX):
-            x_copy(c, d).wait_recv()
-        zbuf[c] = sbuf[c, x] + rx[c, 0] + rx[c, 1] + rx[c, 2]
-        for d in range(1, NZ):
-            z_copy(c, d).start()
-        return 0
-
-    lax.fori_loop(0, chunks, second, 0)
 
     sub8 = lax.broadcasted_iota(jnp.int32, (8, 128), 0)
     lane8 = lax.broadcasted_iota(jnp.int32, (8, 128), 1)
@@ -267,24 +298,26 @@
         jnp.where(even, result[2:4], result[6:8]),
     )
     scaled = chosen * weight
-    most = jnp.max(scaled)
-    least = jnp.min(scaled)
-    rmm[0] = jnp.where(lane8 < 64, most, -least)
+    most = jnp.max(jnp.max(scaled, axis=0, keepdims=True), axis=1, keepdims=True)
+    least = jnp.min(jnp.min(scaled, axis=0, keepdims=True), axis=1, keepdims=True)
+    rmm[0, 0:1] = jnp.where(lane8[0:1] < 64, most, -least)
     for d in range(1, NS):
         m_copy(d).start()
     for d in range(1, NS):
         m_copy(d).wait_recv()
-    top = rmm[0]
-    for d in range(1, NS):
-        top = jnp.maximum(top, rmm[d])
-    highest = jnp.max(jnp.where(lane8 < 64, top, -jnp.inf))
-    lowest = -jnp.max(jnp.where(lane8 < 64, -jnp.inf, top))
+    top = rmm[0, 0:1]
+    for d in range(1, NS):
+        top = jnp.maximum(top, rmm[d, 0:1])
+    highest = top[:, 0:1]
+    lowest = -top[:, 64:65]
     span = highest - lowest + 1e-6
     out_ref[0, 0] = (scaled - lowest) / span * spread
 
     def sent(c, _):
-        for d in range(1, NX):
-            x_copy(c, d).wait_send()
+        for side in (0, 1):
+            far_copy(c, side).wait_send()
+            for part in (0, 1):
+                near_copy(c, side, part).wait_send()
         for d in range(1, NZ):
             z_copy(c, d).wait_send()
         return 0
@@ -318,7 +351,8 @@
             pltpu.VMEM((4, 256, 256), BF16),
             pltpu.VMEM((4, 2, 16, 128), F32),
             pltpu.VMEM((chunks, NX, NZ * CH, 128), F32),
-            pltpu.VMEM((chunks, NX - 1, NZ * CH, 128), F32),
+            pltpu.VMEM((chunks, 2, HALF, 128), F32),
+            pltpu.VMEM((chunks, 2, NZ * CH, 128), F32),
             pltpu.VMEM((chunks, NZ * CH, 128), F32),
             pltpu.VMEM((chunks, NZ - 1, CH, 128), F32),
             pltpu.VMEM((128, 128), F32),
@@ -327,8 +361,10 @@
             pltpu.VMEM((NS, 8, 128), F32),
             dma,
             dma((lats // 128,)),
-            dma((chunks, NX - 1)),
-            dma((chunks, NX - 1)),
+            dma((chunks, 2)),
+            dma((chunks, 2)),
+            dma((chunks, 2, 2)),
+            dma((chunks, 2, 2)),
             dma((chunks, NZ - 1)),
             dma((chunks, NZ - 1)),
             dma((NS - 1,)),

time: 52.4 us -> 50.1 us (0.956)
  Pallas kernels: 50.9 us -> 48.6 us
    pallas_call x1, Pallas kernels: 50.9 us -> 48.6 us  [shards(): pl.pallas_call(functools.partial(kernel, truncation, levels), out_shape=j...]
where the time goes in v3:
time: 50.1 us; the launch traced here: 49.9 us
  Pallas kernels  48.6 us (97%)
  local copies, waits for them, and re-layouts  1.29 us (3%)
    pallas_call x1, Pallas kernels, shards(): pl.pallas_call(functools.partial(kernel, truncation, levels), out_shape=j...  48.6 us
    unnamed x1, local copies, waits for them, and re-layouts  1.29 us

profile of v3, /device:TPU:1, one launch (start us, length us, event | category | flops | bytes accessed | tf_op | source)
XLA Modules:
  0.0 49.9 jit_solution(505710227923112196)
XLA Ops:
  0.0 48.6 %shard_map.73 = f32[1,1,2,649]{3,2,1,0:T(2,128)} custom-call(s32[1280]{0:T(1024)} %band_s.1, s32[16]{0:T(128)} %waves_s.1, s32[32]{0:T(128)} %order_s.1, s32[4]{0:T(128)} %bits_s.1, f32[4]{0:T(128)} %power_s.1, bf16[32,2,80,161]{3,2,1,0:T(8,128)(2,1)} %grid_hbm.1, f32[649,1,1280]{2,1,0:T(1,128)} %bitcast.1), custom_call_target="tpu_custom_call" | custom-call | tf_op jit(solution)/shard_map/pallas_call | solution.py:340
  48.6 1.3 %copy.9 = f32[1,1,2,649]{3,2,1,0:T(2,128)} copy(f32[1,1,2,649]{3,2,1,0:T(2,128)} %shard_map.73) | data formatting | bytes 10384

commit v4 on v3

--- a/solution.py
+++ b/solution.py
@@ -46,16 +46,17 @@
     truncation, levels,
     band_s, waves_s, order_s, bits_s, power_s, grid_hbm, leg_hbm,
     out_ref,
-    gridv, legv, leghi, leglo, xf, w, cs, sbuf, rfar, rx, zbuf, rz, obuf, ybuf, ry, rmm,
-    grid_sem, leg_sem, fs_sem, fr_sem, xs_sem, xr_sem, zs_sem, zr_sem, ys_sem, yr_sem, ms_sem, mr_sem,
+    gridv0, gridv, legv, leghi, leglo, xf, w, cs, sbuf, rfar, rx, zbuf, rz, rz0, sum0, rx0, obuf, ybuf, ry, rmm,
+    grid_sem, leg_sem, fs_sem, fr_sem, xs_sem, xr_sem, x0s_sem, x0r_sem, zs_sem, zr_sem, ys_sem, yr_sem, ms_sem, mr_sem,
 ):
     ew, ns = lax.axis_index("ew"), lax.axis_index("ns")
     x, z = lax.rem(ew, NX), lax.div(ew, NX)
-    rows = gridv.shape[2]
-    points = gridv.shape[3]
+    rows, points = grid_hbm.shape[2:]
     chunks = rows // CH
 
-    grid_copy = pltpu.make_async_copy(grid_hbm, gridv, grid_sem)
+    grid_copy0 = pltpu.make_async_copy(grid_hbm.at[:, :, 0:CH], gridv0, grid_sem.at[0])
+    grid_copy0.start()
+    grid_copy = pltpu.make_async_copy(grid_hbm.at[:, :, CH:rows], gridv, grid_sem.at[1])
     grid_copy.start()
     leg_copies = [
         pltpu.make_async_copy(leg_hbm.at[:, 0, k * 128 : (k + 1) * 128], legv.at[k], leg_sem.at[k])
@@ -90,8 +91,6 @@
     point0 = (first + sub16).astype(F32)
     point_end = (first + points).astype(F32)
 
-    grid_copy.wait()
-
     def neighbour(side):
         return lax.rem(x + (1 if side == 0 else NX - 1), NX)
 
@@ -144,13 +143,13 @@
         for d in range(1, NZ):
             z_copy(c, d).start()
 
-    def chunk(c, _):
+    def compute(c, grid_ref, grid_row):
         def convert(zz, _):
             for xx in range(NX):
                 field = order_s[zz * NX + xx]
                 for h in range(2):
                     at = pl.multiple_of((h * 32 + xx * NZ + zz) * CH, CH)
-                    block = gridv[field, h, pl.ds(pl.multiple_of(c * CH, CH), CH), :].astype(F32)
+                    block = grid_ref[field, h, pl.ds(grid_row, CH), :].astype(F32)
                     xf[0, pl.ds(at, CH), :] = block[:, 0:128]
                     xf[1, pl.ds(at, CH), 0 : points - 128] = block[:, 128:points]
             return 0
@@ -191,31 +190,59 @@
 
         lax.fori_loop(0, CH // 8, half, 0)
 
-        @pl.when(c == 0)
-        def _():
-            pl.semaphore_wait(barrier, NX - 1 + NZ - 1 + NS - 1)
-
+    def first_z_copy(d):
+        to = lax.rem(z + d, NZ)
+        return pltpu.make_async_remote_copy(
+            src_ref=sbuf.at[0, :, pl.ds(pl.multiple_of(to * CH, CH), CH)], dst_ref=rz0.at[d - 1],
+            send_sem=zs_sem.at[0, d - 1], recv_sem=zr_sem.at[0, d - 1],
+            device_id={"ew": to * NX + x}, device_id_type=MESH)
+
+    def first_x_copy(d):
+        to = lax.rem(x + d, NX)
+        return pltpu.make_async_remote_copy(
+            src_ref=sum0.at[to], dst_ref=rx0.at[d - 1],
+            send_sem=x0s_sem.at[d - 1], recv_sem=x0r_sem.at[d - 1],
+            device_id={"ew": z * NX + to}, device_id_type=MESH)
+
+    grid_copy0.wait()
+    compute(0, gridv0, 0)
+    pl.semaphore_wait(barrier, NX - 1 + NZ - 1 + NS - 1)
+    for d in range(1, NZ):
+        first_z_copy(d).start()
+    grid_copy.wait()
+
+    def chunk(c, _):
+        compute(c, gridv, pl.multiple_of(c * CH - CH, CH))
         for side in (0, 1):
             far_copy(c, side).start()
             near_copy(c, side, 1 - side).start()
 
-        @pl.when(c >= 2)
+        @pl.when(c >= 3)
         def _():
             pass_on(c - 2)
 
         return 0
 
-    lax.fori_loop(0, chunks, chunk, 0)
+    lax.fori_loop(1, chunks, chunk, 0)
 
     pass_on(chunks - 2)
-    along_z(0)
+    along_z(1)
     pass_on(chunks - 1)
+    along_z(2)
+    for d in range(1, NZ):
+        first_z_copy(d).wait_recv()
+    total = sbuf[0, :, pl.ds(pl.multiple_of(z * CH, CH), CH), :]
+    for d in range(NZ - 1):
+        total = total + rz0[d]
+    sum0[...] = total
+    for d in range(1, NX):
+        first_x_copy(d).start()
 
     def second(c, _):
         along_z(c)
         return 0
 
-    lax.fori_loop(1, chunks, second, 0)
+    lax.fori_loop(3, chunks, second, 0)
 
     for copy in leg_copies:
         copy.wait()
@@ -234,12 +261,7 @@
     lane8 = lax.broadcasted_iota(jnp.int32, (8, 128), 1)
     obuf[...] = jnp.zeros_like(obuf)
 
-    def third(c, _):
-        for d in range(1, NZ):
-            z_copy(c, d).wait_recv()
-        total = zbuf[c, pl.ds(pl.multiple_of(z * CH, CH), CH)]
-        for d in range(NZ - 1):
-            total = total + rz[c, d]
+    def place(c, total):
         for g in range(CH // 8):
             o = total[g * 8 : g * 8 + 8]
             r = pltpu.roll(o, 4, 0)
@@ -247,9 +269,21 @@
             r = pltpu.roll(pltpu.roll(o, 4, 0), 64, 1)
             o = jnp.where((sub8 < 4) == (lane8 < 64), o, r)
             obuf[pl.ds(pl.multiple_of(c * CH + g * 8, 8), 8), :] = o
+
+    for d in range(1, NX):
+        first_x_copy(d).wait_recv()
+    place(0, sum0[x] + rx0[0] + rx0[1] + rx0[2])
+
+    def third(c, _):
+        for d in range(1, NZ):
+            z_copy(c, d).wait_recv()
+        total = zbuf[c, pl.ds(pl.multiple_of(z * CH, CH), CH)]
+        for d in range(NZ - 1):
+            total = total + rz[c, d]
+        place(c, total)
         return 0
 
-    lax.fori_loop(0, chunks, third, 0)
+    lax.fori_loop(1, chunks, third, 0)
 
     turned = obuf[...].T
     for p in range(NS):
@@ -273,6 +307,20 @@
     weight = jnp.exp(power * jnp.log(degree * (degree + 1.0) + 2.0))
     spread = (lax.shift_left(jnp.int32(1), bits) - 1).astype(F32) * (1.0 / 4096.0)
 
+    def sent(c, _):
+        for side in (0, 1):
+            far_copy(c, side).wait_send()
+            for part in (0, 1):
+                near_copy(c, side, part).wait_send()
+        for d in range(1, NZ):
+            z_copy(c, d).wait_send()
+        return 0
+
+    lax.fori_loop(1, chunks, sent, 0)
+    for d in range(1, NZ):
+        first_z_copy(d).wait_send()
+    for d in range(1, NX):
+        first_x_copy(d).wait_send()
     for d in range(1, NS):
         y_copy(d).wait_recv()
     pieces = [None] * (rows * NS // 128)
@@ -304,6 +352,8 @@
     for d in range(1, NS):
         m_copy(d).start()
     for d in range(1, NS):
+        y_copy(d).wait_send()
+    for d in range(1, NS):
         m_copy(d).wait_recv()
     top = rmm[0, 0:1]
     for d in range(1, NS):
@@ -313,18 +363,7 @@
     span = highest - lowest + 1e-6
     out_ref[0, 0] = (scaled - lowest) / span * spread
 
-    def sent(c, _):
-        for side in (0, 1):
-            far_copy(c, side).wait_send()
-            for part in (0, 1):
-                near_copy(c, side, part).wait_send()
-        for d in range(1, NZ):
-            z_copy(c, d).wait_send()
-        return 0
-
-    lax.fori_loop(0, chunks, sent, 0)
-    for d in range(1, NS):
-        y_copy(d).wait_send()
+    for d in range(1, NS):
         m_copy(d).wait_send()
 
 
@@ -343,7 +382,8 @@
         in_specs=[smem] * 5 + [hbm] * 2,
         out_specs=pl.BlockSpec(memory_space=pltpu.VMEM),
         scratch_shapes=[
-            pltpu.VMEM((fields, hemis, rows, points), BF16),
+            pltpu.VMEM((fields, hemis, CH, points), BF16),
+            pltpu.VMEM((fields, hemis, rows - CH, points), BF16),
             pltpu.VMEM((lats // 128, columns, 128), F32),
             pltpu.VMEM((lats, columns), BF16),
             pltpu.VMEM((lats, columns), BF16),
@@ -355,16 +395,21 @@
             pltpu.VMEM((chunks, 2, NZ * CH, 128), F32),
             pltpu.VMEM((chunks, NZ * CH, 128), F32),
             pltpu.VMEM((chunks, NZ - 1, CH, 128), F32),
+            pltpu.VMEM((NZ - 1, NX, CH, 128), F32),
+            pltpu.VMEM((NX, CH, 128), F32),
+            pltpu.VMEM((NX - 1, CH, 128), F32),
             pltpu.VMEM((128, 128), F32),
             pltpu.VMEM((NS, 8, 128), F32),
             pltpu.VMEM((NS, 8, 128), F32),
             pltpu.VMEM((NS, 8, 128), F32),
-            dma,
+            dma((2,)),
             dma((lats // 128,)),
             dma((chunks, 2)),
             dma((chunks, 2)),
             dma((chunks, 2, 2)),
             dma((chunks, 2, 2)),
+            dma((NX - 1,)),
+            dma((NX - 1,)),
             dma((chunks, NZ - 1)),
             dma((chunks, NZ - 1)),
             dma((NS - 1,)),

time: 50.1 us -> 48.5 us (0.968)
  Pallas kernels: 48.6 us -> 47 us
    pallas_call x1, Pallas kernels: 48.6 us -> 47 us  [shards(): pl.pallas_call(functools.partial(kernel, truncation, levels), out_shape=j...]
where the time goes in v4:
time: 48.5 us; the launch traced here: 48.3 us
  Pallas kernels  47 us (97%)
  local copies, waits for them, and re-layouts  1.29 us (3%)
    pallas_call x1, Pallas kernels, shards(): pl.pallas_call(functools.partial(kernel, truncation, levels), out_shape=j...  47 us
    unnamed x1, local copies, waits for them, and re-layouts  1.29 us

profile of v4, /device:TPU:1, one launch (start us, length us, event | category | flops | bytes accessed | tf_op | source)
XLA Modules:
  0.0 48.3 jit_solution(12831652913370178100)
XLA Ops:
  0.0 47.0 %shard_map.73 = f32[1,1,2,649]{3,2,1,0:T(2,128)} custom-call(s32[1280]{0:T(1024)} %band_s.1, s32[16]{0:T(128)} %waves_s.1, s32[32]{0:T(128)} %order_s.1, s32[4]{0:T(128)} %bits_s.1, f32[4]{0:T(128)} %power_s.1, bf16[32,2,80,161]{3,2,1,0:T(8,128)(2,1)} %grid_hbm.1, f32[649,1,1280]{2,1,0:T(1,128)} %bitcast.1), custom_call_target="tpu_custom_call" | custom-call | tf_op jit(solution)/shard_map/pallas_call | solution.py:379
  47.0 1.3 %copy.9 = f32[1,1,2,649]{3,2,1,0:T(2,128)} copy(f32[1,1,2,649]{3,2,1,0:T(2,128)} %shard_map.73) | data formatting | bytes 10384

commit v5 on v4

--- a/solution.py
+++ b/solution.py
@@ -24,8 +24,8 @@
     return [float(v) for v in cheb.convert(kind=np.polynomial.Polynomial).coef]
 
 
-COS = _fit(lambda t: np.cos(2 * np.pi * t), 8)
-SIN = _fit(lambda t: np.sin(2 * np.pi * t) / t, 8)
+COS = _fit(lambda t: np.cos(2 * np.pi * t), 7)
+SIN = _fit(lambda t: np.sin(2 * np.pi * t) / t, 7)
 
 
 def _horner(coefs, z):
@@ -44,16 +44,24 @@
 
 def kernel(
     truncation, levels,
-    band_s, waves_s, order_s, bits_s, power_s, grid_hbm, leg_hbm,
+    band_hbm, waves_hbm, order_hbm, bits_hbm, power_hbm, grid_hbm, leg_hbm,
     out_ref,
+    band_s, waves_s, order_s, bits_s, power_s,
     gridv0, gridv, legv, leghi, leglo, xf, w, cs, sbuf, rfar, rx, zbuf, rz, rz0, sum0, rx0, obuf, ybuf, ry, rmm,
-    grid_sem, leg_sem, fs_sem, fr_sem, xs_sem, xr_sem, x0s_sem, x0r_sem, zs_sem, zr_sem, ys_sem, yr_sem, ms_sem, mr_sem,
+    small_sem, grid_sem, leg_sem, fs_sem, fr_sem, xs_sem, xr_sem, x0s_sem, x0r_sem, zs_sem, zr_sem, ys_sem, yr_sem, ms_sem, mr_sem,
 ):
     ew, ns = lax.axis_index("ew"), lax.axis_index("ns")
     x, z = lax.rem(ew, NX), lax.div(ew, NX)
     rows, points = grid_hbm.shape[2:]
     chunks = rows // CH
 
+    small_copies = [
+        pltpu.make_async_copy(a, b, small_sem.at[i])
+        for i, (a, b) in enumerate(
+            ((waves_hbm, waves_s), (band_hbm, band_s), (order_hbm, order_s), (bits_hbm, bits_s), (power_hbm, power_s)))
+    ]
+    for copy in small_copies:
+        copy.start()
     grid_copy0 = pltpu.make_async_copy(grid_hbm.at[:, :, 0:CH], gridv0, grid_sem.at[0])
     grid_copy0.start()
     grid_copy = pltpu.make_async_copy(grid_hbm.at[:, :, CH:rows], gridv, grid_sem.at[1])
@@ -75,6 +83,9 @@
 
     w[...] = jnp.zeros_like(w)
     xf[1] = jnp.zeros_like(xf[1])
+
+    for copy in small_copies:
+        copy.wait()
 
     lane = lax.broadcasted_iota(jnp.int32, (16, 128), 1)
     sub16 = lax.broadcasted_iota(jnp.int32, (16, 128), 0)
@@ -193,8 +204,8 @@
     def first_z_copy(d):
         to = lax.rem(z + d, NZ)
         return pltpu.make_async_remote_copy(
-            src_ref=sbuf.at[0, :, pl.ds(pl.multiple_of(to * CH, CH), CH)], dst_ref=rz0.at[d - 1],
-            send_sem=zs_sem.at[0, d - 1], recv_sem=zr_sem.at[0, d - 1],
+            src_ref=sbuf.at[1, :, pl.ds(pl.multiple_of(to * CH, CH), CH)], dst_ref=rz0.at[d - 1],
+            send_sem=zs_sem.at[1, d - 1], recv_sem=zr_sem.at[1, d - 1],
             device_id={"ew": to * NX + x}, device_id_type=MESH)
 
     def first_x_copy(d):
@@ -207,31 +218,36 @@
     grid_copy0.wait()
     compute(0, gridv0, 0)
     pl.semaphore_wait(barrier, NX - 1 + NZ - 1 + NS - 1)
-    for d in range(1, NZ):
-        first_z_copy(d).start()
-    grid_copy.wait()
-
-    def chunk(c, _):
-        compute(c, gridv, pl.multiple_of(c * CH - CH, CH))
+    def send_x(c):
         for side in (0, 1):
             far_copy(c, side).start()
             near_copy(c, side, 1 - side).start()
 
-        @pl.when(c >= 3)
+    send_x(0)
+    grid_copy.wait()
+    compute(1, gridv, 0)
+    for d in range(1, NZ):
+        first_z_copy(d).start()
+
+    def chunk(c, _):
+        compute(c, gridv, pl.multiple_of(c * CH - CH, CH))
+        send_x(c)
+
+        @pl.when(c != 3)
         def _():
             pass_on(c - 2)
 
         return 0
 
-    lax.fori_loop(1, chunks, chunk, 0)
+    lax.fori_loop(2, chunks, chunk, 0)
 
     pass_on(chunks - 2)
-    along_z(1)
+    along_z(0)
     pass_on(chunks - 1)
     along_z(2)
     for d in range(1, NZ):
         first_z_copy(d).wait_recv()
-    total = sbuf[0, :, pl.ds(pl.multiple_of(z * CH, CH), CH), :]
+    total = sbuf[1, :, pl.ds(pl.multiple_of(z * CH, CH), CH), :]
     for d in range(NZ - 1):
         total = total + rz0[d]
     sum0[...] = total
@@ -272,9 +288,10 @@
 
     for d in range(1, NX):
         first_x_copy(d).wait_recv()
-    place(0, sum0[x] + rx0[0] + rx0[1] + rx0[2])
-
-    def third(c, _):
+    place(1, sum0[x] + rx0[0] + rx0[1] + rx0[2])
+
+    def third(i, _):
+        c = i + lax.div(i + 2, 3)
         for d in range(1, NZ):
             z_copy(c, d).wait_recv()
         total = zbuf[c, pl.ds(pl.multiple_of(z * CH, CH), CH)]
@@ -283,7 +300,7 @@
         place(c, total)
         return 0
 
-    lax.fori_loop(1, chunks, third, 0)
+    lax.fori_loop(0, chunks - 1, third, 0)
 
     turned = obuf[...].T
     for p in range(NS):
@@ -307,7 +324,8 @@
     weight = jnp.exp(power * jnp.log(degree * (degree + 1.0) + 2.0))
     spread = (lax.shift_left(jnp.int32(1), bits) - 1).astype(F32) * (1.0 / 4096.0)
 
-    def sent(c, _):
+    def sent(i, _):
+        c = i + lax.div(i + 2, 3)
         for side in (0, 1):
             far_copy(c, side).wait_send()
             for part in (0, 1):
@@ -316,7 +334,7 @@
             z_copy(c, d).wait_send()
         return 0
 
-    lax.fori_loop(1, chunks, sent, 0)
+    lax.fori_loop(0, chunks - 1, sent, 0)
     for d in range(1, NZ):
         first_z_copy(d).wait_send()
     for d in range(1, NX):
@@ -373,15 +391,19 @@
     truncation = columns - 2
     levels = fields // field_bits.shape[0]
     chunks = rows // CH
-    smem = pl.BlockSpec(memory_space=pltpu.SMEM)
     hbm = pl.BlockSpec(memory_space=pltpu.HBM)
     dma = pltpu.SemaphoreType.DMA
     return pl.pallas_call(
         functools.partial(kernel, truncation, levels),
         out_shape=jax.ShapeDtypeStruct((1, 1, 2, columns), F32),
-        in_specs=[smem] * 5 + [hbm] * 2,
+        in_specs=[hbm] * 7,
         out_specs=pl.BlockSpec(memory_space=pltpu.VMEM),
         scratch_shapes=[
+            pltpu.SMEM(band_rows.shape, jnp.int32),
+            pltpu.SMEM(wave_pairs.shape, jnp.int32),
+            pltpu.SMEM(packer_order.shape, jnp.int32),
+            pltpu.SMEM(field_bits.shape, jnp.int32),
+            pltpu.SMEM(field_power.shape, F32),
             pltpu.VMEM((fields, hemis, CH, points), BF16),
             pltpu.VMEM((fields, hemis, rows - CH, points), BF16),
             pltpu.VMEM((lats // 128, columns, 128), F32),
@@ -402,6 +424,7 @@
             pltpu.VMEM((NS, 8, 128), F32),
             pltpu.VMEM((NS, 8, 128), F32),
             pltpu.VMEM((NS, 8, 128), F32),
+            dma((5,)),
             dma((2,)),
             dma((lats // 128,)),
             dma((chunks, 2)),

time: 48.5 us -> 47.3 us (0.975)
  Pallas kernels: 47 us -> 45.9 us
    pallas_call x1, Pallas kernels: 47 us -> 45.9 us  [shards(): pl.pallas_call(functools.partial(kernel, truncation, levels), out_shape=j...]
where the time goes in v5:
time: 47.3 us; the launch traced here: 47.1 us
  Pallas kernels  45.9 us (97%)
  local copies, waits for them, and re-layouts  1.29 us (3%)
    pallas_call x1, Pallas kernels, shards(): pl.pallas_call(functools.partial(kernel, truncation, levels), out_shape=j...  45.9 us
    unnamed x1, local copies, waits for them, and re-layouts  1.29 us

profile of v5, /device:TPU:1, one launch (start us, length us, event | category | flops | bytes accessed | tf_op | source)
XLA Modules:
  0.0 47.1 jit_solution(2645513425185157145)
XLA Ops:
  0.0 45.9 %shard_map.73 = f32[1,1,2,649]{3,2,1,0:T(2,128)} custom-call(s32[1280]{0:T(1024)} %band_hbm.1, s32[16]{0:T(128)} %waves_hbm.1, s32[32]{0:T(128)} %order_hbm.1, s32[4]{0:T(128)} %bits_hbm.1, f32[4]{0:T(128)} %power_hbm.1, bf16[32,2,80,161]{3,2,1,0:T(8,128)(2,1)} %grid_hbm.1, f32[649,1,1280]{2,1,0:T(1,128)} %bitcast.1), custom_call_target="tpu_custom_call" | custom-call | tf_op jit(solution)/shard_map/pallas_call | solution.py:396
  45.9 1.3 %copy.9 = f32[1,1,2,649]{3,2,1,0:T(2,128)} copy(f32[1,1,2,649]{3,2,1,0:T(2,128)} %shard_map.73) | data formatting | bytes 10384

commit v6 on v5

--- a/solution.py
+++ b/solution.py
@@ -14,6 +14,8 @@
 NS = 16
 CH = 16
 HALF = NZ * CH // 2
+FAR_Z = (4, 3, 5, 2, 6, 1, 7)
+FAR_NS = (8, 7, 9, 6, 10, 5, 11, 4, 12, 3, 13, 2, 14, 1, 15)
 F32 = jnp.float32
 BF16 = jnp.bfloat16
 
@@ -74,12 +76,12 @@
         copy.start()
 
     barrier = pltpu.get_barrier_semaphore()
+    for d in FAR_NS:
+        pl.semaphore_signal(barrier, inc=1, device_id={"ns": lax.rem(ns + d, NS)}, device_id_type=MESH)
+    for d in FAR_Z:
+        pl.semaphore_signal(barrier, inc=1, device_id={"ew": lax.rem(z + d, NZ) * NX + x}, device_id_type=MESH)
     for d in range(1, NX):
         pl.semaphore_signal(barrier, inc=1, device_id={"ew": z * NX + lax.rem(x + d, NX)}, device_id_type=MESH)
-    for d in range(1, NZ):
-        pl.semaphore_signal(barrier, inc=1, device_id={"ew": lax.rem(z + d, NZ) * NX + x}, device_id_type=MESH)
-    for d in range(1, NS):
-        pl.semaphore_signal(barrier, inc=1, device_id={"ns": lax.rem(ns + d, NS)}, device_id_type=MESH)
 
     w[...] = jnp.zeros_like(w)
     xf[1] = jnp.zeros_like(xf[1])
@@ -151,7 +153,7 @@
             for part in (0, 1):
                 near_copy(c, side, part).wait_recv()
         zbuf[c] = sbuf[c, x] + rx[c, 0] + rx[c, 1]
-        for d in range(1, NZ):
+        for d in FAR_Z:
             z_copy(c, d).start()
 
     def compute(c, grid_ref, grid_row):
@@ -226,7 +228,7 @@
     send_x(0)
     grid_copy.wait()
     compute(1, gridv, 0)
-    for d in range(1, NZ):
+    for d in FAR_Z:
         first_z_copy(d).start()
 
     def chunk(c, _):
@@ -305,7 +307,7 @@
     turned = obuf[...].T
     for p in range(NS):
         ybuf[p] = jnp.concatenate([turned[4 * p : 4 * p + 4], turned[64 + 4 * p : 68 + 4 * p]], 0)
-    for d in range(1, NS):
+    for d in FAR_NS:
         y_copy(d).start()
     ry[ns] = ybuf[ns]
 
@@ -367,7 +369,7 @@
     most = jnp.max(jnp.max(scaled, axis=0, keepdims=True), axis=1, keepdims=True)
     least = jnp.min(jnp.min(scaled, axis=0, keepdims=True), axis=1, keepdims=True)
     rmm[0, 0:1] = jnp.where(lane8[0:1] < 64, most, -least)
-    for d in range(1, NS):
+    for d in FAR_NS:
         m_copy(d).start()
     for d in range(1, NS):
         y_copy(d).wait_send()

time: 47.3 us -> 46.7 us (0.987)
  Pallas kernels: 45.9 us -> 45.3 us
    pallas_call x1, Pallas kernels: 45.9 us -> 45.3 us  [shards(): pl.pallas_call(functools.partial(kernel, truncation, levels), out_shape=j...]
where the time goes in v6:
time: 46.7 us; the launch traced here: 46.6 us
  Pallas kernels  45.3 us (97%)
  local copies, waits for them, and re-layouts  1.29 us (3%)
    pallas_call x1, Pallas kernels, shards(): pl.pallas_call(functools.partial(kernel, truncation, levels), out_shape=j...  45.3 us
    unnamed x1, local copies, waits for them, and re-layouts  1.29 us

profile of v6, /device:TPU:1, one launch (start us, length us, event | category | flops | bytes accessed | tf_op | source)
XLA Modules:
  0.0 46.6 jit_solution(11697804367885711607)
XLA Ops:
  0.0 45.3 %shard_map.73 = f32[1,1,2,649]{3,2,1,0:T(2,128)} custom-call(s32[1280]{0:T(1024)} %band_hbm.1, s32[16]{0:T(128)} %waves_hbm.1, s32[32]{0:T(128)} %order_hbm.1, s32[4]{0:T(128)} %bits_hbm.1, f32[4]{0:T(128)} %power_hbm.1, bf16[32,2,80,161]{3,2,1,0:T(8,128)(2,1)} %grid_hbm.1, f32[649,1,1280]{2,1,0:T(1,128)} %bitcast.1), custom_call_target="tpu_custom_call" | custom-call | tf_op jit(solution)/shard_map/pallas_call | solution.py:398
  45.3 1.3 %copy.9 = f32[1,1,2,649]{3,2,1,0:T(2,128)} copy(f32[1,1,2,649]{3,2,1,0:T(2,128)} %shard_map.73) | data formatting | bytes 10384

commit v7 on v6

--- a/solution.py
+++ b/solution.py
@@ -206,8 +206,8 @@
     def first_z_copy(d):
         to = lax.rem(z + d, NZ)
         return pltpu.make_async_remote_copy(
-            src_ref=sbuf.at[1, :, pl.ds(pl.multiple_of(to * CH, CH), CH)], dst_ref=rz0.at[d - 1],
-            send_sem=zs_sem.at[1, d - 1], recv_sem=zr_sem.at[1, d - 1],
+            src_ref=sbuf.at[2, :, pl.ds(pl.multiple_of(to * CH, CH), CH)], dst_ref=rz0.at[d - 1],
+            send_sem=zs_sem.at[2, d - 1], recv_sem=zr_sem.at[2, d - 1],
             device_id={"ew": to * NX + x}, device_id_type=MESH)
 
     def first_x_copy(d):
@@ -228,6 +228,8 @@
     send_x(0)
     grid_copy.wait()
     compute(1, gridv, 0)
+    send_x(1)
+    compute(2, gridv, CH)
     for d in FAR_Z:
         first_z_copy(d).start()
 
@@ -235,21 +237,19 @@
         compute(c, gridv, pl.multiple_of(c * CH - CH, CH))
         send_x(c)
 
-        @pl.when(c != 3)
-        def _():
-            pass_on(c - 2)
+        pass_on(c - 3)
 
         return 0
 
-    lax.fori_loop(2, chunks, chunk, 0)
+    lax.fori_loop(3, chunks, chunk, 0)
 
     pass_on(chunks - 2)
     along_z(0)
     pass_on(chunks - 1)
-    along_z(2)
+    along_z(1)
     for d in range(1, NZ):
         first_z_copy(d).wait_recv()
-    total = sbuf[1, :, pl.ds(pl.multiple_of(z * CH, CH), CH), :]
+    total = sbuf[2, :, pl.ds(pl.multiple_of(z * CH, CH), CH), :]
     for d in range(NZ - 1):
         total = total + rz0[d]
     sum0[...] = total
@@ -290,10 +290,10 @@
 
     for d in range(1, NX):
         first_x_copy(d).wait_recv()
-    place(1, sum0[x] + rx0[0] + rx0[1] + rx0[2])
+    place(2, sum0[x] + rx0[0] + rx0[1] + rx0[2])
 
     def third(i, _):
-        c = i + lax.div(i + 2, 3)
+        c = i + lax.div(i, 2)
         for d in range(1, NZ):
             z_copy(c, d).wait_recv()
         total = zbuf[c, pl.ds(pl.multiple_of(z * CH, CH), CH)]
@@ -327,7 +327,7 @@
     spread = (lax.shift_left(jnp.int32(1), bits) - 1).astype(F32) * (1.0 / 4096.0)
 
     def sent(i, _):
-        c = i + lax.div(i + 2, 3)
+        c = i + lax.div(i, 2)
         for side in (0, 1):
             far_copy(c, side).wait_send()
             for part in (0, 1):

time: 46.7 us -> 46.5 us (level)
  no operation moved by 1% of the time
where the time goes in v7:
time: 46.5 us; the launch traced here: 46.4 us
  Pallas kernels  45.1 us (97%)
  local copies, waits for them, and re-layouts  1.29 us (3%)
    pallas_call x1, Pallas kernels, shards(): pl.pallas_call(functools.partial(kernel, truncation, levels), out_shape=j...  45.1 us
    unnamed x1, local copies, waits for them, and re-layouts  1.29 us

profile of v7, /device:TPU:1, one launch (start us, length us, event | category | flops | bytes accessed | tf_op | source)
XLA Modules:
  0.0 46.4 jit_solution(1769818309754620364)
XLA Ops:
  0.0 45.1 %shard_map.73 = f32[1,1,2,649]{3,2,1,0:T(2,128)} custom-call(s32[1280]{0:T(1024)} %band_hbm.1, s32[16]{0:T(128)} %waves_hbm.1, s32[32]{0:T(128)} %order_hbm.1, s32[4]{0:T(128)} %bits_hbm.1, f32[4]{0:T(128)} %power_hbm.1, bf16[32,2,80,161]{3,2,1,0:T(8,128)(2,1)} %grid_hbm.1, f32[649,1,1280]{2,1,0:T(1,128)} %bitcast.1), custom_call_target="tpu_custom_call" | custom-call | tf_op jit(solution)/shard_map/pallas_call | solution.py:398
  45.1 1.3 %copy.9 = f32[1,1,2,649]{3,2,1,0:T(2,128)} copy(f32[1,1,2,649]{3,2,1,0:T(2,128)} %shard_map.73) | data formatting | bytes 10384

commit v8 on v7

--- a/solution.py
+++ b/solution.py
@@ -247,6 +247,7 @@
     along_z(0)
     pass_on(chunks - 1)
     along_z(1)
+    along_z(3)
     for d in range(1, NZ):
         first_z_copy(d).wait_recv()
     total = sbuf[2, :, pl.ds(pl.multiple_of(z * CH, CH), CH), :]
@@ -260,7 +261,7 @@
         along_z(c)
         return 0
 
-    lax.fori_loop(3, chunks, second, 0)
+    lax.fori_loop(4, chunks, second, 0)
 
     for copy in leg_copies:
         copy.wait()

time: 46.5 us -> 46.5 us (level)
  no operation moved by 1% of the time
where the time goes in v8:
time: 46.5 us; the launch traced here: 46.4 us
  Pallas kernels  45.1 us (97%)
  local copies, waits for them, and re-layouts  1.29 us (3%)
    pallas_call x1, Pallas kernels, shards(): pl.pallas_call(functools.partial(kernel, truncation, levels), out_shape=j...  45.1 us
    unnamed x1, local copies, waits for them, and re-layouts  1.29 us

profile of v8, /device:TPU:1, one launch (start us, length us, event | category | flops | bytes accessed | tf_op | source)
XLA Modules:
  0.0 46.4 jit_solution(9545413804968930024)
XLA Ops:
  0.0 45.1 %shard_map.73 = f32[1,1,2,649]{3,2,1,0:T(2,128)} custom-call(s32[1280]{0:T(1024)} %band_hbm.1, s32[16]{0:T(128)} %waves_hbm.1, s32[32]{0:T(128)} %order_hbm.1, s32[4]{0:T(128)} %bits_hbm.1, f32[4]{0:T(128)} %power_hbm.1, bf16[32,2,80,161]{3,2,1,0:T(8,128)(2,1)} %grid_hbm.1, f32[649,1,1280]{2,1,0:T(1,128)} %bitcast.1), custom_call_target="tpu_custom_call" | custom-call | tf_op jit(solution)/shard_map/pallas_call | solution.py:399
  45.1 1.3 %copy.9 = f32[1,1,2,649]{3,2,1,0:T(2,128)} copy(f32[1,1,2,649]{3,2,1,0:T(2,128)} %shard_map.73) | data formatting | bytes 10384
